TPU v7x, 128 devices: a whole 4x4x4 slice. The times are simulated.
128 devices in a mesh: row: 2 (over x_hi), col: 64 (over x_lo, y, z, core).
Axes of the slice: x: 4 (x_hi: 2, x_lo: 2; x = x_hi * 2 + x_lo), y: 4, z: 4, core: 2. Of those that a mesh axis runs over, the one named last changes fastest.
Arguments:
- tokens: bfloat16 [2, 24576, 768], P('row', 'col'), may hold values from -6 to 6
- attn_gain: bfloat16 [768], replicated, may hold values from 0.099609375 to 1.8984375
- query_weight: bfloat16 [768, 768], replicated, may hold values from -0.21875 to 0.21875
- key_weight: bfloat16 [768, 768], replicated, may hold values from -0.21875 to 0.21875
- value_weight: bfloat16 [768, 768], replicated, may hold values from -0.21875 to 0.21875
- output_weight: bfloat16 [768, 768], replicated, may hold values from -2.5 to 2.5
- ffn_gain: bfloat16 [768], replicated, may hold values from 0.099609375 to 1.8984375
- gate_weight: bfloat16 [768, 2048], replicated, may hold values from -0.21875 to 0.21875
- up_weight: bfloat16 [768, 2048], replicated, may hold values from -0.21875 to 0.21875
- down_weight: bfloat16 [2048, 768], replicated, may hold values from -0.125 to 0.125
- relative_table: bfloat16 [32, 12], replicated, may hold values from -3 to 3
- layout_table: bfloat16 [32, 12], replicated, may hold values from -3 to 3
- cotangent: bfloat16 [2, 24576, 768], P('row', 'col'), may hold values from -6 to 6
- rel_bucket: int32 [2, 24576, 768], P('row', 'col'), may hold values from 0 to 32, as said below
- layout_bucket: int32 [2, 24576, 768], P('row', 'col'), may hold values from 0 to 31
- halo_index: int32 [2, 64, 4, 96], P('row', 'col'), may hold values from -1 to 383, as said below
Outputs:
- layer_out: bfloat16 [2, 24576, 768], P('row', 'col')
- input_grad: bfloat16 [2, 24576, 768], P('row', 'col')
- attn_gain_grad: float32 [768], replicated
- query_grad: float32 [768, 768], replicated
- key_grad: float32 [768, 768], replicated
- value_grad: float32 [768, 768], replicated
- output_grad: float32 [768, 768], replicated
- ffn_gain_grad: float32 [768], replicated
- gate_grad: float32 [768, 2048], replicated
- up_grad: float32 [768, 2048], replicated
- down_grad: float32 [2048, 768], replicated
- relative_grad: float32 [32, 12], replicated
- layout_grad: float32 [32, 12], replicated
Inputs may be any that keep to these rules, and one draw needn't show every extreme that they name: `halo_index`: block [r, c, d] lists the tokens of region (r, c) that the neighbour in direction d reads (0: next row, 1: previous row, 2: next column, 3: previous column): between 48 and 96 distinct indices first, then -1; some block is full and some holds exactly 48 indices. `rel_bucket`: for a query of region (r, c), slots below 384 are its own region's tokens (never marked); then four blocks of 96 slots follow the order of the key window. The value 32 marks a slot that is no key: a missing region, a region of another page, or a -1 of the sender's block; pages cover both rows and 2 or 4 neighbouring columns.
All inputs are finite; a program needn't handle non-finite values.
Results may differ from a plain program's by a relative error of at most 0.015.
Values may be sent and summed in bfloat16 or wider, within the bound.
No kernel may reach another device: no remote copies, remote signals or barrier semaphores. Data moves between devices by JAX's collectives and lax.ppermute only.
A program may use at most 256 MiB of HBM per device.

v0:
```python
import jax
import jax.numpy as jnp
from jax import lax
from jax.sharding import PartitionSpec as P

EPS = 1e-06
NEG = -1000000000.0


def from_behind(value, axis, steps):
    count = lax.axis_size(axis)
    initial, last = (max(0, -steps), min(count, count - steps))
    return lax.ppermute(value, axis, [(source, source + steps) for source in range(initial, last)])


def shortened(shard):
    return jax.tree.map(lambda a: a.astype(jnp.bfloat16) if a.dtype == jnp.float32 else a, shard)


def matmul_tn(left, right):
    return lax.dot_general(
        left, right, (((0,), (0,)), ((), ())), preferred_element_type=jnp.float32
    )


def matmul_nt(left, right):
    return lax.dot_general(
        left, right, (((1,), (1,)), ((), ())), preferred_element_type=jnp.float32
    )


def norm_forward(value, gain):
    inverse = lax.rsqrt(jnp.mean(value * value, axis=-1, keepdims=True) + EPS)
    return (inverse, value * inverse * gain)


def norm_backward(grad_normed, value, inverse, gain):
    gain_grad = jnp.sum(grad_normed * value * inverse, axis=0)
    scaled = grad_normed * gain
    cubed = inverse * inverse * inverse
    value_grad = inverse * scaled - value * cubed * jnp.mean(scaled * value, axis=-1, keepdims=True)
    return (value_grad, gain_grad)


def gated(gate, up_part):
    return jax.nn.gelu(gate, approximate=True) * up_part


def scores_of(query_heads, key_heads, bias, valid, scale):
    raw = (
        jnp.einsum("qhd,khd->hqk", query_heads, key_heads, preferred_element_type=jnp.float32)
        * scale
    )
    return jnp.where(valid[None], raw + bias, NEG)


def body(
    tokens,
    attn_gain,
    query_weight,
    key_weight,
    value_weight,
    output_weight,
    ffn_gain,
    gate_weight,
    up_weight,
    down_weight,
    relative_table,
    layout_table,
    cotangent,
    rel_bucket,
    layout_bucket,
    halo_index,
):
    rows = tokens.shape[1]
    width = tokens.shape[2]
    heads = relative_table.shape[1]
    head_size = width // heads
    scale = head_size ** (-0.5)
    halo = halo_index.shape[3]
    resid = tokens[0].astype(jnp.float32)
    gain_one = attn_gain.astype(jnp.float32)
    gain_two = ffn_gain.astype(jnp.float32)
    inverse_one, normed_one = norm_forward(resid, gain_one)
    normed_one = normed_one.astype(jnp.bfloat16)
    query = jnp.dot(normed_one, query_weight, preferred_element_type=jnp.float32).astype(
        jnp.bfloat16
    )
    keys = jnp.dot(normed_one, key_weight, preferred_element_type=jnp.float32).astype(jnp.bfloat16)
    values = jnp.dot(normed_one, value_weight, preferred_element_type=jnp.float32).astype(
        jnp.bfloat16
    )
    picks = jnp.maximum(halo_index[0, 0], 0)
    send_keys = keys[picks]
    send_values = values[picks]
    lower = from_behind((send_keys[0], send_values[0]), "row", 1)
    upper = from_behind((send_keys[1], send_values[1]), "row", -1)
    left = from_behind((send_keys[2], send_values[2]), "col", 1)
    right = from_behind((send_keys[3], send_values[3]), "col", -1)
    key_win = jnp.concatenate([keys, lower[0], upper[0], left[0], right[0]], axis=0).reshape(
        -1, heads, head_size
    )
    value_win = jnp.concatenate([values, lower[1], upper[1], left[1], right[1]], axis=0).reshape(
        -1, heads, head_size
    )
    query_heads = query.reshape(rows, heads, head_size)
    relative = rel_bucket[0]
    valid = relative < relative_table.shape[0]
    rel_onehot = jax.nn.one_hot(relative, relative_table.shape[0], dtype=jnp.bfloat16)
    lay_onehot = jax.nn.one_hot(layout_bucket[0], layout_table.shape[0], dtype=jnp.bfloat16)
    bias = jnp.einsum("qkb,bh->hqk", rel_onehot, relative_table, preferred_element_type=jnp.float32)
    bias = bias + jnp.einsum(
        "qkb,bh->hqk", lay_onehot, layout_table, preferred_element_type=jnp.float32
    )
    logits = scores_of(query_heads, key_win, bias, valid, scale)
    highest = jnp.max(logits, axis=-1, keepdims=True)
    powered = jnp.exp(logits - highest)
    summed_exp = jnp.sum(powered, axis=-1, keepdims=True)
    probs_low = (powered / summed_exp).astype(jnp.bfloat16)
    log_total = highest + jnp.log(summed_exp)
    attended = jnp.einsum("hqk,khd->qhd", probs_low, value_win, preferred_element_type=jnp.float32)
    attended = attended.reshape(rows, width).astype(jnp.bfloat16)
    middle = resid + jnp.dot(attended, output_weight, preferred_element_type=jnp.float32)
    inverse_two, normed_two = norm_forward(middle, gain_two)
    normed_two = normed_two.astype(jnp.bfloat16)
    gate = jnp.dot(normed_two, gate_weight, preferred_element_type=jnp.float32)
    up_part = jnp.dot(normed_two, up_weight, preferred_element_type=jnp.float32)
    mixed = gated(gate, up_part).astype(jnp.bfloat16)
    layer_out = (middle + jnp.dot(mixed, down_weight, preferred_element_type=jnp.float32)).astype(
        jnp.bfloat16
    )
    grad_out = cotangent[0]
    down_grad = matmul_tn(mixed, grad_out)
    d_mixed = matmul_nt(grad_out, down_weight)
    _, gelu_pullback = jax.vjp(gated, gate, up_part)
    d_gate, d_up = gelu_pullback(d_mixed)
    d_gate = d_gate.astype(jnp.bfloat16)
    d_up = d_up.astype(jnp.bfloat16)
    gate_grad = matmul_tn(normed_two, d_gate)
    up_grad = matmul_tn(normed_two, d_up)
    d_normed_two = matmul_nt(d_gate, gate_weight) + matmul_nt(d_up, up_weight)
    d_middle, ffn_gain_grad = norm_backward(d_normed_two, middle, inverse_two, gain_two)
    d_middle = d_middle + grad_out.astype(jnp.float32)
    d_branch = d_middle.astype(jnp.bfloat16)
    output_grad = matmul_tn(attended, d_branch)
    d_attended = (
        matmul_nt(d_branch, output_weight).astype(jnp.bfloat16).reshape(rows, heads, head_size)
    )
    logits = scores_of(query_heads, key_win, bias, valid, scale)
    probs = jnp.exp(logits - log_total)
    d_probs = jnp.einsum("qhd,khd->hqk", d_attended, value_win, preferred_element_type=jnp.float32)
    d_logits = (probs * (d_probs - jnp.sum(probs * d_probs, axis=-1, keepdims=True))).astype(
        jnp.bfloat16
    )
    relative_grad = jnp.einsum(
        "qkb,hqk->bh", rel_onehot, d_logits, preferred_element_type=jnp.float32
    )
    layout_grad = jnp.einsum(
        "qkb,hqk->bh", lay_onehot, d_logits, preferred_element_type=jnp.float32
    )
    d_query = (
        jnp.einsum("hqk,khd->qhd", d_logits, key_win, preferred_element_type=jnp.float32) * scale
    )
    d_query = d_query.reshape(rows, width).astype(jnp.bfloat16)
    d_key_win = (
        jnp.einsum("hqk,qhd->khd", d_logits, query_heads, preferred_element_type=jnp.float32)
        * scale
    ).reshape(-1, width)
    d_value_win = jnp.einsum(
        "hqk,qhd->khd", probs.astype(jnp.bfloat16), d_attended, preferred_element_type=jnp.float32
    ).reshape(-1, width)

    def block_of(number):
        begin = rows + number * halo
        return (d_key_win[begin : begin + halo], d_value_win[begin : begin + halo])

    back_lower = from_behind(shortened(block_of(0)), "row", -1)
    back_upper = from_behind(shortened(block_of(1)), "row", 1)
    back_left = from_behind(shortened(block_of(2)), "col", -1)
    back_right = from_behind(shortened(block_of(3)), "col", 1)
    d_keys = d_key_win[:rows]
    d_values = d_value_win[:rows]
    for number, returned in enumerate((back_lower, back_upper, back_left, back_right)):
        d_keys = d_keys.at[picks[number]].add(returned[0])
        d_values = d_values.at[picks[number]].add(returned[1])
    d_keys = d_keys.astype(jnp.bfloat16)
    d_values = d_values.astype(jnp.bfloat16)
    query_grad = matmul_tn(normed_one, d_query)
    key_grad = matmul_tn(normed_one, d_keys)
    value_grad = matmul_tn(normed_one, d_values)
    d_normed_one = (
        matmul_nt(d_query, query_weight)
        + matmul_nt(d_keys, key_weight)
        + matmul_nt(d_values, value_weight)
    )
    d_resid, attn_gain_grad = norm_backward(d_normed_one, resid, inverse_one, gain_one)
    input_grad = (d_middle + d_resid).astype(jnp.bfloat16)
    totals = lax.psum(
        (
            attn_gain_grad,
            query_grad,
            key_grad,
            value_grad,
            output_grad,
            ffn_gain_grad,
            gate_grad,
            up_grad,
            down_grad,
            relative_grad,
            layout_grad,
        ),
        ("row", "col"),
    )
    attn_gain_grad, query_grad, key_grad, value_grad, output_grad, ffn_gain_grad = totals[:6]
    gate_grad, up_grad, down_grad, relative_grad, layout_grad = totals[6:]
    return (
        layer_out[None],
        input_grad[None],
        attn_gain_grad,
        query_grad,
        key_grad,
        value_grad,
        output_grad,
        ffn_gain_grad,
        gate_grad,
        up_grad,
        down_grad,
        relative_grad,
        layout_grad,
    )


def solution(mesh):
    return jax.shard_map(
        body,
        mesh=mesh,
        in_specs=(
            P("row", "col", None),
            P(),
            P(),
            P(),
            P(),
            P(),
            P(),
            P(),
            P(),
            P(),
            P(),
            P(),
            P("row", "col", None),
            P("row", "col", None),
            P("row", "col", None),
            P("row", "col", None, None),
        ),
        out_specs=(
            P("row", "col", None),
            P("row", "col", None),
            P(),
            P(),
            P(),
            P(),
            P(),
            P(),
            P(),
            P(),
            P(),
            P(),
            P(),
        ),
        check_vma=False,
    )
```

profile of v0, /device:TPU:1, one launch (start us, length us, event | category | flops | bytes accessed | tf_op | source)
XLA Modules:
  0.0 610.3 jit_solution(4580795668847193872)
XLA Ops:
  10.8 3.1 constant_dynamic-update-slice_fusion.4
  13.9 4.2 gather_fusion
  20.1 6.1 %collective-permute-start = (bf16[96,768]{1,0:T(8,128)(2,1)}, bf16[96,768]{1,0:T(8,128)(2,1)}, u32[]{:S(2)}, u32[]{:S(2)}) collective-permute-start(bf16[96,768]{1,0:T(8,128)(2,1)} %get-tuple-element.46), channel_id=1, source_target_pairs={{0,64},{1,65},{2,66},{3,67},{4,68},{5,69},{6,70},{7,71},{8,72},{9,... | collective-permute-start | bytes 442376 | tf_op jit(solution)/shard_map/ppermute | solution.py:13
  27.5 4.4 collective-permute-start.2
  33.8 3.0 constant_dynamic-update-slice_fusion.9
  36.8 4.2 gather_fusion.1
  43.0 7.2 %collective-permute-start.4 = (bf16[96,768]{1,0:T(8,128)(2,1)}, bf16[96,768]{1,0:T(8,128)(2,1)}, u32[]{:S(2)}, u32[]{:S(2)}) collective-permute-start(bf16[96,768]{1,0:T(8,128)(2,1)} %get-tuple-element.42), channel_id=1, source_target_pairs={{0,64},{1,65},{2,66},{3,67},{4,68},{5,69},{6,70},{7,71},{8,72},{9,... | collective-permute-start | bytes 442376 | tf_op jit(solution)/shard_map/ppermute | solution.py:13
  55.7 3.0 convolution_convert_fusion.2
  58.8 9.4 %fusion.3 = f32[384,768,12]{0,2,1:T(8,128)} fusion(s32[384,768]{0,1:T(8,128)S(1)} %copy-done.17, bf16[32,12]{0,1:T(8,128)(2,1)S(1)} %copy-done.41), kind=kOutput, calls=%fused_computation.15 | convolution fusion | flops 235929600 | bytes 15336192 | tf_op jit(solution)/shard_map/qkb,bh->hqk/dot_general | solution.py:111
  68.2 9.4 %fusion.1 = f32[384,768,12]{0,2,1:T(8,128)} fusion(s32[384,768]{0,1:T(8,128)S(1)} %copy-done.15, bf16[32,12]{0,1:T(8,128)(2,1)S(1)} %copy-done.42), kind=kOutput, calls=%fused_computation.12 | convolution fusion | flops 235929600 | bytes 15336192 | tf_op jit(solution)/shard_map/qkb,bh->hqk/dot_general | solution.py:112
  78.0 17.5 %copy.52 = f32[384,768,12]{1,0,2:T(8,128)} copy(f32[384,768,12]{0,2,1:T(8,128)} %fusion.3) | data formatting | bytes 28311552 | tf_op jit(solution)/shard_map/qkb,bh->hqk/dot_general | solution.py:111
  95.5 17.4 %copy.53 = f32[384,768,12]{1,0,2:T(8,128)} copy(f32[384,768,12]{0,2,1:T(8,128)} %fusion.1) | data formatting | bytes 28311552 | tf_op jit(solution)/shard_map/qkb,bh->hqk/dot_general | solution.py:112
  117.9 3.9 collective-permute-start.6
  139.0 18.7 %fusion.99 = (f32[12,384]{1,0:T(8,128)S(1)}, f32[12,384,768]{2,1,0:T(8,128)}) fusion(f32[384,768,12]{1,0,2:T(8,128)} %copy.52, f32[384,768,12]{1,0,2:T(8,128)} %copy.53, bf16[384,12,64]{0,2,1:T(8,128)(2,1)} %bitcast.162, bf16[768,12,64]{0,2,1:T(8,128)(2,1)} %bitcast.160, pred[384,768]{1,0:T(8,128)(4,1)S(1)} %compare_bitcast_fusion), kind=kOutput, calls=%fused_computation.154 | convolution fusion | flops 470674944 | bytes 44550144 | tf_op jit(solution)/shard_map/qhd,khd->hqk/dot_general | solution.py:51
  157.7 7.6 %fusion.9 = f32[12,384]{1,0:T(8,128)S(1)} fusion(f32[12,384,768]{2,1,0:T(8,128)} %get-tuple-element.60, f32[12,384]{1,0:T(8,128)S(1)} %get-tuple-element.59), kind=kLoop, calls=%fused_computation.27 | loop fusion | flops 7073280 | bytes 14192640 | tf_op jit(solution)/shard_map/reduce_sum | solution.py:118
  166.8 4.8 fusion.33
  177.7 5.1 multiply_convert_fusion.1
  191.2 14.4 %multiply_reduce_fusion = (f32[12,384]{1,0:T(8,128)S(1)}, f32[12,384,768]{2,1,0:T(8,128)}) fusion(f32[12,384,768]{2,1,0:T(8,128)} %get-tuple-element.60, f32[12,384]{1,0:T(8,128)S(1)} %log_add_fusion, bf16[384,12,64]{0,2,1:T(8,128)(2,1)} %bitcast.172, bf16[768,12,64]{0,2,1:T(8,128)(2,1)} %bitcast.174), kind=kOutput, calls=%fused_computation.23 | convolution fusion | flops 463597056 | bytes 30117888 | tf_op jit(solution)/shard_map/qhd,khd->hqk/dot_general | solution.py:151
  205.7 6.9 %multiply_convert_fusion = bf16[12,384,768]{2,1,0:T(8,128)(2,1)S(1)} fusion(f32[12,384,768]{2,1,0:T(8,128)} %get-tuple-element.65, f32[12,384,768]{2,1,0:T(8,128)S(1)} %bitcast.159, f32[12,384]{1,0:T(8,128)S(1)} %get-tuple-element.64, f32[12,384]{1,0:T(8,128)S(1)} %log_add_fusion), kind=kLoop, calls=%fused_computation.22 | loop fusion | flops 14155776 | bytes 35426304 | tf_op jit(solution)/shard_map/convert_element_type | solution.py:152
  212.6 3.1 fusion.32
  218.6 4.3 fusion.101
  225.1 4.5 fusion.106
  229.6 4.5 fusion.107
  239.8 7.1 %collective-permute-start.9 = (bf16[96,768]{1,0:T(8,128)(2,1)}, bf16[96,768]{1,0:T(8,128)(2,1)}, u32[]{:S(2)}, u32[]{:S(2)}) collective-permute-start(bf16[96,768]{1,0:T(8,128)(2,1)} %copy.57), channel_id=1, source_target_pairs={{0,64},{1,65},{2,66},{3,67},{4,68},{5,69},{6,70},{7,71},{8,72},{9,... | collective-permute-start | bytes 442376 | tf_op jit(solution)/shard_map/ppermute | solution.py:13
  250.4 3.9 collective-permute-start.11
  259.6 6.2 %fusion.53 = f32[2048,768]{1,0:T(8,128)} fusion(bf16[384,2048]{1,0:T(8,128)(2,1)} %get-tuple-element.30, bf16[1,384,768]{2,1,0:T(8,128)(2,1)} %param.28), kind=kOutput, calls=%fused_computation.90 | convolution fusion | flops 1207959552 | bytes 8454144 | tf_op jit(solution)/shard_map/dot_general | solution.py:21
  279.6 6.9 %collective-permute-start.13 = (bf16[96,768]{1,0:T(8,128)(2,1)}, bf16[96,768]{1,0:T(8,128)(2,1)}, u32[]{:S(2)}, u32[]{:S(2)}) collective-permute-start(bf16[96,768]{1,0:T(8,128)(2,1)} %copy.62), channel_id=1, source_target_pairs={{0,64},{1,65},{2,66},{3,67},{4,68},{5,69},{6,70},{7,71},{8,72},{9,... | collective-permute-start | bytes 442376 | tf_op jit(solution)/shard_map/ppermute | solution.py:13
  286.5 3.9 scatter_custom_fusion
  292.3 3.9 scatter_custom_fusion.1
  296.2 3.6 collective-permute-start.15
  299.9 3.9 scatter_custom_fusion.2
  303.8 3.9 scatter_custom_fusion.3
  307.7 3.8 fusion.70
  311.5 3.9 scatter_custom_fusion.4
  315.4 3.9 scatter_custom_fusion.5
  319.2 3.9 scatter_custom_fusion.6
  323.1 3.9 scatter_custom_fusion.7
  327.0 3.8 fusion.59
  330.8 13.5 %copy.65 = bf16[12,384,768]{1,0,2:T(8,128)(2,1)} copy(bf16[12,384,768]{2,1,0:T(8,128)(2,1)} %copy-done.2) | data formatting | bytes 14155776 | tf_op jit(solution)/shard_map/convert_element_type | solution.py:152
  346.6 5.3 fusion.34
  351.9 5.6 fusion.47
  357.5 5.8 fusion.48
  367.2 77.2 %all-reduce = (f32[768]{0:T(1024)}, f32[768]{0:T(1024)}, f32[32,12]{0,1:T(8,128)}, f32[32,12]{0,1:T(8,128)}) all-reduce(f32[768]{0:T(1024)S(1)} %get-tuple-element.15, f32[768]{0:T(1024)S(1)} %get-tuple-element.13, f32[32,12]{0,1:T(8,128)S(1)} %fusion.47, f32[32,12]{0,1:T(8,128)S(1)} %fusion.48), channel_id=1, replica_groups=mesh['row'=2,'col'=64] {'row','col'}, use_global_device_ids=true, to_apply=%region_16.17 | all-reduce | flops 2304 | bytes 18432 | tf_op jit(solution)/shard_map/psum | solution.py:198
  444.4 3.0 fusion.52
  447.4 135.3 %all-reduce.4.cloned.1.call-done = (f32[768,768]{1,0:T(8,128)}, f32[768,768]{1,0:T(8,128)}, f32[768,768]{1,0:T(8,128)}, f32[768,768]{1,0:T(8,128)}, f32[768,2048...) async-done(((f32[768,768]{1,0:T(8,128)}, f32[768,768]{1,0:T(8,128)}, f32[768,768]{1,0:T(8,128)}, f32[768,768]{1,0:T(8,128)}, f32[768,2048]{1,0:T(8,128)}, ...) | async-done | bytes 28311568 | tf_op jit(solution)/shard_map/psum | solution.py:198
  582.7 3.4 copy.96
  592.1 3.2 copy.100
  596.7 2.9 copy.101
  (203 shorter events, 106.8 us)
Async XLA Ops:
  7.2 170.5 %copy-start = (bf16[2048,768]{1,0:T(8,128)(2,1)S(1)}, bf16[2048,768]{1,0:T(8,128)(2,1)}, u32[]{:S(2)}) copy-start(bf16[2048,768]{1,0:T(8,128)(2,1)} %param.25) | copy-start | bytes 9437188
  7.2 575.5 %all-reduce.4.cloned.1.call-start = ((), (), s32[]{:S(2)}) async-start(), calls=%async_computation | async-start | bytes 56623104 | tf_op jit(solution)/shard_map/psum | solution.py:198
  18.1 15.8 %copy-start.3 = (bf16[1,384,768]{2,1,0:T(8,128)(2,1)S(1)}, bf16[1,384,768]{2,1,0:T(8,128)(2,1)}, u32[]{:S(2)}) copy-start(bf16[1,384,768]{2,1,0:T(8,128)(2,1)} %param.16) | copy-start | bytes 1769476
  20.1 95.0 %collective-permute-start = (bf16[96,768]{1,0:T(8,128)(2,1)}, bf16[96,768]{1,0:T(8,128)(2,1)}, u32[]{:S(2)}, u32[]{:S(2)}) collective-permute-start(bf16[96,768]{1,0:T(8,128)(2,1)} %get-tuple-element.46), channel_id=1, source_target_pairs={{0,64},{1,65},{2,66},{3,67},{4,68},{5,69},{6,70},{7,71},{8,72},{9,... | collective-permute-start | bytes 442376 | tf_op jit(solution)/shard_map/ppermute | solution.py:13
  26.2 91.7 %collective-permute-start.1 = (bf16[96,768]{1,0:T(8,128)(2,1)}, bf16[96,768]{1,0:T(8,128)(2,1)}, u32[]{:S(2)}, u32[]{:S(2)}) collective-permute-start(bf16[96,768]{1,0:T(8,128)(2,1)} %get-tuple-element.45), channel_id=1, source_target_pairs={{64,0},{65,1},{66,2},{67,3},{68,4},{69,5},{70,6},{71,7},{72,8},{73... | collective-permute-start | bytes 442376 | tf_op jit(solution)/shard_map/ppermute | solution.py:13
  27.5 96.0 %collective-permute-start.2 = (bf16[96,768]{1,0:T(8,128)(2,1)}, bf16[96,768]{1,0:T(8,128)(2,1)}, u32[]{:S(2)}, u32[]{:S(2)}) collective-permute-start(bf16[96,768]{1,0:T(8,128)(2,1)} %get-tuple-element.44), channel_id=1, source_target_pairs={{0,1},{1,2},{2,3},{3,4},{4,5},{5,6},{6,7},{7,8},{8,9},{9,10},{10,1... | collective-permute-start | bytes 442376 | tf_op jit(solution)/shard_map/ppermute | solution.py:13
  31.9 95.3 %collective-permute-start.3 = (bf16[96,768]{1,0:T(8,128)(2,1)}, bf16[96,768]{1,0:T(8,128)(2,1)}, u32[]{:S(2)}, u32[]{:S(2)}) collective-permute-start(bf16[96,768]{1,0:T(8,128)(2,1)} %get-tuple-element.43), channel_id=1, source_target_pairs={{1,0},{2,1},{3,2},{4,3},{5,4},{6,5},{7,6},{8,7},{9,8},{10,9},{11,1... | collective-permute-start | bytes 442376 | tf_op jit(solution)/shard_map/ppermute | solution.py:13
  40.9 9.3 %copy-start.25 = (s32[1,384,768]{2,1,0:T(8,128)S(1)}, s32[1,384,768]{2,1,0:T(8,128)}, u32[]{:S(2)}) copy-start(s32[1,384,768]{2,1,0:T(8,128)} %param.29) | copy-start | bytes 3538948
  43.0 85.8 %collective-permute-start.4 = (bf16[96,768]{1,0:T(8,128)(2,1)}, bf16[96,768]{1,0:T(8,128)(2,1)}, u32[]{:S(2)}, u32[]{:S(2)}) collective-permute-start(bf16[96,768]{1,0:T(8,128)(2,1)} %get-tuple-element.42), channel_id=1, source_target_pairs={{0,64},{1,65},{2,66},{3,67},{4,68},{5,69},{6,70},{7,71},{8,72},{9,... | collective-permute-start | bytes 442376 | tf_op jit(solution)/shard_map/ppermute | solution.py:13
  58.7 9.4 %copy-start.15 = (s32[384,768]{0,1:T(8,128)S(1)}, s32[384,768]{0,1:T(8,128)}, u32[]{:S(2)}) copy-start(s32[384,768]{0,1:T(8,128)} %copy.50) | copy-start | bytes 3538948
  58.7 9.4 %copy-start.42 = (bf16[32,12]{0,1:T(8,128)(2,1)S(1)}, bf16[32,12]{0,1:T(8,128)(2,1)}, u32[]{:S(2)}) copy-start(bf16[32,12]{0,1:T(8,128)(2,1)} %param.27) | copy-start | bytes 2308
  115.0 15.3 %collective-permute-start.5 = (bf16[96,768]{1,0:T(8,128)(2,1)}, bf16[96,768]{1,0:T(8,128)(2,1)S(1)}, u32[]{:S(2)}, u32[]{:S(2)}) collective-permute-start(bf16[96,768]{1,0:T(8,128)(2,1)} %get-tuple-element.41), channel_id=1, source_target_pairs={{64,0},{65,1},{66,2},{67,3},{68,4},{69,5},{70,6},{71,7},{72,8},{73... | collective-permute-start | bytes 442376 | tf_op jit(solution)/shard_map/ppermute | solution.py:13
  117.9 15.5 %collective-permute-start.6 = (bf16[96,768]{1,0:T(8,128)(2,1)}, bf16[96,768]{1,0:T(8,128)(2,1)}, u32[]{:S(2)}, u32[]{:S(2)}) collective-permute-start(bf16[96,768]{1,0:T(8,128)(2,1)} %get-tuple-element.40), channel_id=1, source_target_pairs={{0,1},{1,2},{2,3},{3,4},{4,5},{5,6},{6,7},{7,8},{8,9},{9,10},{10,1... | collective-permute-start | bytes 442376 | tf_op jit(solution)/shard_map/ppermute | solution.py:13
  123.4 11.6 %collective-permute-start.7 = (bf16[96,768]{1,0:T(8,128)(2,1)}, bf16[96,768]{1,0:T(8,128)(2,1)}, u32[]{:S(2)}, u32[]{:S(2)}) collective-permute-start(bf16[96,768]{1,0:T(8,128)(2,1)} %get-tuple-element.39), channel_id=1, source_target_pairs={{1,0},{2,1},{3,2},{4,3},{5,4},{6,5},{7,6},{8,7},{9,8},{10,9},{11,1... | collective-permute-start | bytes 442376 | tf_op jit(solution)/shard_map/ppermute | solution.py:13
  139.0 26.3 %copy-start.23 = (bf16[768,768]{0,1:T(8,128)(2,1)S(1)}, bf16[768,768]{0,1:T(8,128)(2,1)}, u32[]{:S(2)}) copy-start(bf16[768,768]{0,1:T(8,128)(2,1)} %copy.45) | copy-start | bytes 3538948
  157.7 9.2 %copy-start.1 = (f32[12,384,768]{2,1,0:T(8,128)S(1)}, f32[12,384,768]{2,1,0:T(8,128)}, u32[]{:S(2)}) copy-start(f32[12,384,768]{2,1,0:T(8,128)} %get-tuple-element.60) | copy-start | bytes 42467332
  166.8 4.8 copy-start.4
  166.8 4.8 copy-start.34
  172.5 13.7 %copy-start.24 = (f32[384,768]{1,0:T(8,128)}, f32[384,768]{1,0:T(8,128)S(1)}, u32[]{:S(2)}) copy-start(f32[384,768]{1,0:T(8,128)S(1)} %get-tuple-element.62) | copy-start | bytes 3538948
  191.2 14.4 %slice-start = ((s8[14155776]{0:T(1024)(128)(4,1)}), s8[4194304]{0:T(1024)(128)(4,1)S(1)}, s32[]{:S(2)}) async-start(s8[14155776]{0:T(1024)(128)(4,1)} %bitcast.158), calls=%async_computation.1 | async-start | bytes 8388608
  191.2 14.4 %slice-start.1 = ((s8[14155776]{0:T(1024)(128)(4,1)}), s8[4194304]{0:T(1024)(128)(4,1)S(1)}, s32[]{:S(2)}) async-start(s8[14155776]{0:T(1024)(128)(4,1)} %bitcast.158), calls=%async_computation.2 | async-start | bytes 8388608
  191.2 14.4 %slice-start.2 = ((s8[14155776]{0:T(1024)(128)(4,1)}), s8[4194304]{0:T(1024)(128)(4,1)S(1)}, s32[]{:S(2)}) async-start(s8[14155776]{0:T(1024)(128)(4,1)} %bitcast.158), calls=%async_computation.3 | async-start | bytes 8388608
  191.2 14.4 %slice-start.3 = ((s8[14155776]{0:T(1024)(128)(4,1)}), s8[1572864]{0:T(1024)(128)(4,1)S(1)}, s32[]{:S(2)}) async-start(s8[14155776]{0:T(1024)(128)(4,1)} %bitcast.158), calls=%async_computation.4 | async-start | bytes 3145728
  205.6 6.9 %copy-start.10 = (bf16[768,768]{0,1:T(8,128)(2,1)S(1)}, bf16[768,768]{0,1:T(8,128)(2,1)}, u32[]{:S(2)}) copy-start(bf16[768,768]{0,1:T(8,128)(2,1)} %copy.47) | copy-start | bytes 3538948
  225.1 4.5 copy-start.31
  236.8 42.8 %collective-permute-start.8 = (bf16[96,768]{1,0:T(8,128)(2,1)}, bf16[96,768]{1,0:T(8,128)(2,1)}, u32[]{:S(2)}, u32[]{:S(2)}) collective-permute-start(bf16[96,768]{1,0:T(8,128)(2,1)} %copy.55), channel_id=1, source_target_pairs={{64,0},{65,1},{66,2},{67,3},{68,4},{69,5},{70,6},{71,7},{72,8},{73... | collective-permute-start | bytes 442376 | tf_op jit(solution)/shard_map/ppermute | solution.py:13
  239.8 50.6 %collective-permute-start.9 = (bf16[96,768]{1,0:T(8,128)(2,1)}, bf16[96,768]{1,0:T(8,128)(2,1)}, u32[]{:S(2)}, u32[]{:S(2)}) collective-permute-start(bf16[96,768]{1,0:T(8,128)(2,1)} %copy.57), channel_id=1, source_target_pairs={{0,64},{1,65},{2,66},{3,67},{4,68},{5,69},{6,70},{7,71},{8,72},{9,... | collective-permute-start | bytes 442376 | tf_op jit(solution)/shard_map/ppermute | solution.py:13
  247.7 48.5 %collective-permute-start.10 = (bf16[96,768]{1,0:T(8,128)(2,1)}, bf16[96,768]{1,0:T(8,128)(2,1)}, u32[]{:S(2)}, u32[]{:S(2)}) collective-permute-start(bf16[96,768]{1,0:T(8,128)(2,1)} %copy.58), channel_id=1, source_target_pairs={{1,0},{2,1},{3,2},{4,3},{5,4},{6,5},{7,6},{8,7},{9,8},{10,9},{11,1... | collective-permute-start | bytes 442376 | tf_op jit(solution)/shard_map/ppermute | solution.py:13
  250.4 53.4 %collective-permute-start.11 = (bf16[96,768]{1,0:T(8,128)(2,1)}, bf16[96,768]{1,0:T(8,128)(2,1)}, u32[]{:S(2)}, u32[]{:S(2)}) collective-permute-start(bf16[96,768]{1,0:T(8,128)(2,1)} %copy.59), channel_id=1, source_target_pairs={{0,1},{1,2},{2,3},{3,4},{4,5},{5,6},{6,7},{7,8},{8,9},{9,10},{10,1... | collective-permute-start | bytes 442376 | tf_op jit(solution)/shard_map/ppermute | solution.py:13
  258.3 53.2 %collective-permute-start.12 = (bf16[96,768]{1,0:T(8,128)(2,1)}, bf16[96,768]{1,0:T(8,128)(2,1)}, u32[]{:S(2)}, u32[]{:S(2)}) collective-permute-start(bf16[96,768]{1,0:T(8,128)(2,1)} %copy.60), channel_id=1, source_target_pairs={{64,0},{65,1},{66,2},{67,3},{68,4},{69,5},{70,6},{71,7},{72,8},{73... | collective-permute-start | bytes 442376 | tf_op jit(solution)/shard_map/ppermute | solution.py:13
  259.5 6.2 %copy-start.5 = (bf16[1,384,768]{2,1,0:T(8,128)(2,1)S(1)}, bf16[1,384,768]{2,1,0:T(8,128)(2,1)}, u32[]{:S(2)}) copy-start(bf16[1,384,768]{2,1,0:T(8,128)(2,1)} %param.16) | copy-start | bytes 1769476
  259.6 6.2 %copy-start.21 = (bf16[12,64,384]{2,1,0:T(8,128)(2,1)S(1)}, bf16[12,64,384]{2,1,0:T(8,128)(2,1)}, u32[]{:S(2)}) copy-start(bf16[12,64,384]{2,1,0:T(8,128)(2,1)} %fusion.32) | copy-start | bytes 1769476
  279.6 10.8 %copy-start.39 = (bf16[96,768]{1,0:T(8,128)(2,1)S(1)}, bf16[96,768]{1,0:T(8,128)(2,1)}, u32[]{:S(2)}) copy-start(bf16[96,768]{1,0:T(8,128)(2,1)} %copy.63) | copy-start | bytes 442372
  279.6 35.8 %collective-permute-start.13 = (bf16[96,768]{1,0:T(8,128)(2,1)}, bf16[96,768]{1,0:T(8,128)(2,1)}, u32[]{:S(2)}, u32[]{:S(2)}) collective-permute-start(bf16[96,768]{1,0:T(8,128)(2,1)} %copy.62), channel_id=1, source_target_pairs={{0,64},{1,65},{2,66},{3,67},{4,68},{5,69},{6,70},{7,71},{8,72},{9,... | collective-permute-start | bytes 442376 | tf_op jit(solution)/shard_map/ppermute | solution.py:13
  290.4 28.8 %collective-permute-start.14 = (bf16[96,768]{1,0:T(8,128)(2,1)S(1)}, bf16[96,768]{1,0:T(8,128)(2,1)}, u32[]{:S(2)}, u32[]{:S(2)}) collective-permute-start(bf16[96,768]{1,0:T(8,128)(2,1)S(1)} %copy-done.39), channel_id=1, source_target_pairs={{1,0},{2,1},{3,2},{4,3},{5,4},{6,5},{7,6},{8,7},{9,8},{10,9},{11,1... | collective-permute-start | bytes 442376 | tf_op jit(solution)/shard_map/ppermute | solution.py:13
  296.2 26.9 %collective-permute-start.15 = (bf16[96,768]{1,0:T(8,128)(2,1)S(1)}, bf16[96,768]{1,0:T(8,128)(2,1)}, u32[]{:S(2)}, u32[]{:S(2)}) collective-permute-start(bf16[96,768]{1,0:T(8,128)(2,1)S(1)} %copy.64), channel_id=1, source_target_pairs={{0,1},{1,2},{2,3},{3,4},{4,5},{5,6},{6,7},{7,8},{8,9},{9,10},{10,1... | collective-permute-start | bytes 442376 | tf_op jit(solution)/shard_map/ppermute | solution.py:13
  344.3 7.6 %copy-start.13 = (bf16[12,384,768]{1,0,2:T(8,128)(2,1)S(1)}, bf16[12,384,768]{1,0,2:T(8,128)(2,1)}, u32[]{:S(2)}) copy-start(bf16[12,384,768]{1,0,2:T(8,128)(2,1)} %copy.65) | copy-start | bytes 21233668
  346.6 5.3 copy-start.18
  351.9 5.6 copy-start.16
  357.5 5.9 copy-start.12
  357.5 5.9 copy-start.35
  365.3 79.1 %copy-start.40 = (f32[384]{0:T(512)S(1)}, f32[384]{0:T(512)}, u32[]{:S(2)}) copy-start(f32[384]{0:T(512)} %get-tuple-element.47) | copy-start | bytes 4612
  582.7 4.8 copy-start.28
  586.1 6.0 slice-start.8
  587.5 4.6 slice-start.9
  590.7 4.7 slice-start.6
  592.1 4.6 slice-start.7
  592.1 7.5 %slice-start.4 = ((s8[6291456]{0:T(1024)(128)(4,1)}), s8[4194304]{0:T(1024)(128)(4,1)S(1)}, s32[]{:S(2)}) async-start(s8[6291456]{0:T(1024)(128)(4,1)} %bitcast.164), calls=%async_computation.5 | async-start | bytes 8388608
  (25 other events, 59.8 us)
Sparse Core Ops, SparseCore 0:
  330.9 251.7 all-reduce.3
where the time goes:
time: 617 us; the launch traced here: 610 us
  matrix products  138 us (22%)
  local copies, waits for them, and re-layouts  135 us (22%)
  waiting for transfers between devices  135 us (22%)
  blocking collectives  77.2 us (13%)
  starting transfers between devices  56.3 us (9%)
  other arithmetic  53.2 us (9%)
  between operations  15.1 us (2%)
    psum x1, waiting for transfers between devices, body(): lax.psum((attn_gain_grad, query_grad, key_grad, value_grad, output_grad,...  135 us
    psum x1, blocking collectives, body(): lax.psum((attn_gain_grad, query_grad, key_grad, value_grad, output_grad,...  77.2 us
    ppermute x16, starting transfers between devices, from_behind(): lax.ppermute(value, axis, [(source, source + steps) for source in range(i...  56.3 us
    unnamed x125, local copies, waits for them, and re-layouts  35.3 us
    dot_general x7, matrix products, matmul_tn(): lax.dot_general(left, right, (((0,), (0,)), ((), ())), preferred_element_...  27.3 us
    dot_general x1, matrix products, scores_of(): jnp.einsum('qhd,khd->hqk', query_heads, key_heads, preferred_element_type...  18.7 us
    dot_general x1, local copies, waits for them, and re-layouts, body(): jnp.einsum('qkb,bh->hqk', rel_onehot, relative_table, preferred_element_t...  17.5 us
    dot_general x1, local copies, waits for them, and re-layouts, body(): jnp.einsum('qkb,bh->hqk', lay_onehot, layout_table, preferred_element_typ...  17.4 us
  transfers between devices with their start and end apart: 17, of which 1 were waited for; matrix products, arithmetic and copies ran while one was open for 30% of the time, Pallas kernels for 0%

commit v1 on v0

v1 whole, which is shorter than its diff:
```python
import jax
import jax.numpy as jnp
from jax import lax
from jax.experimental import pallas as pl
from jax.experimental.pallas import tpu as pltpu
from jax.sharding import PartitionSpec as P

BF = jnp.bfloat16
F32 = jnp.float32
EPS = 1e-06
LOG2E = 1.4426950408889634
VMEM_BYTES = 56 * 2**20
REGION = 384
WIDTH = 768
WINDOW = 768
HEADS = 12
HALO = 96
FF = 2048


def params():
    return pltpu.CompilerParams(vmem_limit_bytes=VMEM_BYTES)


def cost(flops, moved, transcendentals=0):
    return pl.CostEstimate(flops=flops, bytes_accessed=moved, transcendentals=transcendentals)


def smem():
    return pl.BlockSpec(memory_space=pltpu.SMEM)


def whole(shape):
    return pl.BlockSpec(shape, lambda *_: (0,) * len(shape))


def mm(a, b):
    return jnp.dot(a, b, preferred_element_type=F32)


def mm_nt(a, b):
    return lax.dot_general(a, b, (((1,), (1,)), ((), ())), preferred_element_type=F32)


def mm_tn(a, b):
    return lax.dot_general(a, b, (((0,), (0,)), ((), ())), preferred_element_type=F32)


def struct(shape, dtype=BF):
    return jax.ShapeDtypeStruct(shape, dtype)


def norm_kernel(place, tokens, gain, index, normed, send_row, send_core, send_chip):
    value = tokens[...].astype(F32)
    inverse = lax.rsqrt(jnp.mean(value * value, axis=-1, keepdims=True) + EPS)
    low = (value * inverse * gain[...].astype(F32)).astype(BF)
    normed[...] = low
    row, odd = place[0], place[1]
    for out, block in ((send_row, row), (send_core, 2 + odd), (send_chip, 3 - odd)):
        picks = index[pl.ds(block, 1), :]
        chosen = lax.broadcasted_iota(jnp.int32, (REGION, HALO), 0) == picks
        out[...] = mm_tn(jnp.where(chosen, 1.0, 0.0).astype(BF), low).astype(BF)


def norm_call(place, tokens, gain, index):
    return pl.pallas_call(
        norm_kernel,
        out_shape=(struct((REGION, WIDTH)),) + (struct((HALO, WIDTH)),) * 3,
        in_specs=[smem()] + [pl.BlockSpec(memory_space=pltpu.VMEM)] * 3,
        out_specs=(pl.BlockSpec(memory_space=pltpu.VMEM),) * 4,
        compiler_params=params(),
        cost_estimate=cost(700_000_000, 2_000_000),
        name="norm_one",
    )(place, tokens, gain, index)


STEP = 2.0**-11
SHIFT = 9000


def bias_kernel(table, relative, layout, out):
    rows = relative.shape[0]

    def look(words, low, bit3, bit4):
        four = [jnp.take_along_axis(words[k], low, axis=0) for k in range(4)]
        return jnp.where(
            bit4, jnp.where(bit3, four[3], four[2]), jnp.where(bit3, four[1], four[0])
        )

    def step(number, carry):
        begin = pl.multiple_of(number * 8, 8)
        for tile in range(WINDOW // 128):
            lanes = slice(tile * 128, tile * 128 + 128)
            rel = relative[pl.ds(begin, 8), lanes]
            lay = layout[pl.ds(begin, 8), lanes]
            rel_low, lay_low = rel & 7, lay & 7
            rel3, rel4 = (rel & 8) != 0, (rel & 16) != 0
            lay3, lay4 = (lay & 8) != 0, (lay & 16) != 0
            masked = rel >= 32
            for pair in range(HEADS // 2):
                words = [table[pair * 8 + k] for k in range(8)]
                word = look(words[:4], rel_low, rel3, rel4) + look(words[4:], lay_low, lay3, lay4)
                high = (word >> 16).astype(F32) * STEP
                low = (word & 0xFFFF).astype(F32) * STEP - 2 * SHIFT * STEP
                out[2 * pair, pl.ds(begin, 8), lanes] = jnp.where(masked, -1.5e9, high)
                out[2 * pair + 1, pl.ds(begin, 8), lanes] = jnp.where(masked, -1.5e9, low)
        return carry

    lax.fori_loop(0, rows // 8, step, 0)


def bias_call(table, relative, layout):
    block = 128
    return pl.pallas_call(
        bias_kernel,
        grid=(REGION // block,),
        out_shape=struct((HEADS, REGION, WINDOW), F32),
        in_specs=[
            whole((48, 8, 128)),
            pl.BlockSpec((block, WINDOW), lambda i: (i, 0)),
            pl.BlockSpec((block, WINDOW), lambda i: (i, 0)),
        ],
        out_specs=pl.BlockSpec((HEADS, block, WINDOW), lambda i: (0, i, 0)),
        compiler_params=params(),
        cost_estimate=cost(100_000_000, 17_000_000),
        name="bias",
    )(table, relative, layout)


def packed_table(relative_table, layout_table):
    def words(table):
        fixed = jnp.round(table.astype(F32) * (LOG2E / STEP)).astype(jnp.int32)
        packed = fixed[:, 0::2] * 65536 + (fixed[:, 1::2] + SHIFT)
        return packed.T.reshape(HEADS // 2, 4, 8)

    both = jnp.concatenate([words(relative_table), words(layout_table)], axis=1)
    return jnp.broadcast_to(both.reshape(48, 8, 1), (48, 8, 128))


def attend_kernel(
    place, normed, from_row, from_core, from_chip, wq, wk, wv, bias,
    window, query, keys, values, probs, attended, scores,
):
    width = wq.shape[1]

    @pl.when(pl.program_id(0) == 0)
    def _():
        row, odd = place[0], place[1]
        window[:REGION] = normed[...]
        window[REGION : REGION + 2 * HALO] = jnp.zeros((2 * HALO, WIDTH), BF)
        window[pl.ds(pl.multiple_of(REGION + HALO - HALO * row, HALO), HALO)] = from_row[...]
        window[pl.ds(pl.multiple_of(REGION + 3 * HALO - HALO * odd, HALO), HALO)] = from_core[...]
        window[pl.ds(pl.multiple_of(REGION + 2 * HALO + HALO * odd, HALO), HALO)] = from_chip[...]

    rows = window[...]
    query[...] = mm(rows[:REGION], wq[...]).astype(BF)
    keys[...] = mm(rows, wk[...]).astype(BF)
    values[...] = mm(rows, wv[...]).astype(BF)
    lane = lax.broadcasted_iota(jnp.int32, (REGION, 128), 1)
    for pair in range(width // 128):
        lanes = slice(pair * 128, pair * 128 + 128)
        halves = []
        for half in range(2):
            head = 2 * pair + half
            mine = (lane < 64) if half == 0 else (lane >= 64)
            one = jnp.where(mine, query[:, lanes], jnp.zeros((), BF))
            slot = head % 2
            scores[slot] = mm_nt(one, keys[:, lanes])
            for begin in range(0, REGION, 32):
                part = slice(begin, begin + 32)
                logits = scores[slot, part] * (0.125 * LOG2E) + bias[head, part]
                highest = jnp.max(logits, axis=-1, keepdims=True)
                powered = jnp.exp2(logits - highest)
                total = jnp.sum(powered, axis=-1, keepdims=True)
                probs[head, part] = (powered * (1.0 / total)).astype(BF)
            halves.append(mm(probs[head], values[:, lanes]))
        attended[:, lanes] = jnp.where(lane < 64, halves[0], halves[1]).astype(BF)


def attend_call(place, normed, from_row, from_core, from_chip, wq, wk, wv, bias, group):
    count = HEADS // group
    width = group * 64
    cols = lambda rows: pl.BlockSpec((rows, width), lambda g: (0, g))
    return pl.pallas_call(
        attend_kernel,
        grid=(count,),
        out_shape=(
            struct((WINDOW, WIDTH)),
            struct((REGION, WIDTH)),
            struct((WINDOW, WIDTH)),
            struct((WINDOW, WIDTH)),
            struct((HEADS, REGION, WINDOW)),
            struct((REGION, WIDTH)),
        ),
        in_specs=[smem(), whole((REGION, WIDTH))]
        + [whole((HALO, WIDTH))] * 3
        + [cols(WIDTH)] * 3
        + [pl.BlockSpec((group, REGION, WINDOW), lambda g: (g, 0, 0))],
        out_specs=(
            whole((WINDOW, WIDTH)),
            cols(REGION),
            cols(WINDOW),
            cols(WINDOW),
            pl.BlockSpec((group, REGION, WINDOW), lambda g: (g, 0, 0)),
            cols(REGION),
        ),
        scratch_shapes=[pltpu.VMEM((2, REGION, WINDOW), F32)],
        compiler_params=params(),
        cost_estimate=cost(3_500_000_000, 30_000_000, 3_600_000),
        name="attend",
    )(place, normed, from_row, from_core, from_chip, wq, wk, wv, bias)


SHARDS = 128
HALF = 64
TILE = 512
PIECE = 16


def tile_of(step, ids):
    core = ids[0] >> 6
    return jnp.where(step < 2, 1 - core, core) * 2 + (step & 1)


def ffn_kernel(
    ids, tokens, attended, wo, gain, cotangent, wg, wu, wd,
    layer_out, d_middle, d_attended, out_grad, gain_grad,
    gate_send, gate_keep, up_send, up_keep, down_send, down_keep,
    middle, normed, normed_t, total_out, total_back,
):
    step = pl.program_id(0)

    def inverse_of(value):
        return lax.rsqrt(jnp.mean(value * value, axis=-1, keepdims=True) + EPS)

    @pl.when(step == 0)
    def _():
        value = tokens[...].astype(F32) + mm(attended[...], wo[...])
        middle[...] = value
        low = (value * inverse_of(value) * gain[...].astype(F32)).astype(BF)
        normed[...] = low
        normed_t[...] = low.T
        total_out[...] = value
        total_back[...] = jnp.zeros_like(total_back)

    low = normed[...]
    grad_out = cotangent[...]
    gate = mm(low, wg[...])
    up_part = mm(low, wu[...])
    cube = gate * gate * gate
    curve = jnp.tanh(0.7978845608 * (gate + 0.044715 * cube))
    half_up = 0.5 * (1.0 + curve)
    act = gate * half_up
    slope = half_up + 0.5 * gate * (1.0 - curve * curve) * (
        0.7978845608 + (3 * 0.7978845608 * 0.044715) * gate * gate
    )
    mixed = (act * up_part).astype(BF)
    d_mixed = mm_nt(grad_out, wd[...])
    d_gate = (d_mixed * up_part * slope).astype(BF)
    d_up = (d_mixed * act).astype(BF)
    total_out[...] += mm(mixed, wd[...])
    total_back[...] += mm_nt(d_gate, wg[...]) + mm_nt(d_up, wu[...])
    gate_grad = mm(normed_t[...], d_gate).astype(BF)
    up_grad = mm(normed_t[...], d_up).astype(BF)
    down_grad = mm_tn(mixed, grad_out).astype(BF)

    def put(gate_out, up_out, down_out):
        flips = [ids[k] & 31 for k in range(3)]
        for piece in range(32):
            col, row = piece // 16, piece % 16
            for third in range(3):
                rows = slice(row * 48 + third * 16, row * 48 + third * 16 + 16)
                cols = slice(col * 256, col * 256 + 256)
                lanes = slice(third * 256, third * 256 + 256)
                gate_out[piece ^ flips[0], :, lanes] = gate_grad[rows, cols]
                up_out[piece ^ flips[1], :, lanes] = up_grad[rows, cols]
            down_out[piece ^ flips[2]] = down_grad[piece * 16 : piece * 16 + 16]

    @pl.when(step < 2)
    def _():
        put(gate_send, up_send, down_send)

    @pl.when(step >= 2)
    def _():
        put(gate_keep, up_keep, down_keep)

    @pl.when(step == 3)
    def _():
        layer_out[...] = total_out[...].astype(BF)
        value = middle[...]
        inverse = inverse_of(value)
        back = total_back[...]
        gain_grad[...] = jnp.sum(back * value * inverse, axis=0, keepdims=True)
        scaled = back * gain[...].astype(F32)
        shared = jnp.mean(scaled * value, axis=-1, keepdims=True)
        whole_grad = (
            grad_out.astype(F32) + inverse * scaled - value * (inverse * inverse * inverse) * shared
        )
        d_middle[...] = whole_grad
        branch = whole_grad.astype(BF)
        out_grad[...] = mm_tn(attended[...], branch).astype(BF)
        d_attended[...] = mm_nt(branch, wo[...]).astype(BF)


def ffn_call(ids, tokens, attended, wo, gain, cotangent, wg, wu, wd):
    block = (32, PIECE, WIDTH)

    def sent(k):
        def index(g, ids):
            return (jnp.where(g < 2, g & 1, 1) ^ ((ids[k] >> 5) & 1), 0, 0)
        return pl.BlockSpec(block, index)

    def kept(k):
        def index(g, ids):
            return (jnp.where(g < 2, 0, g & 1) ^ ((ids[k] >> 5) & 1), 0, 0)
        return pl.BlockSpec(block, index)

    cols = pl.BlockSpec((WIDTH, TILE), lambda g, ids: (0, tile_of(g, ids)))
    half = struct((HALF, PIECE, WIDTH))
    return pl.pallas_call(
        ffn_kernel,
        grid_spec=pltpu.PrefetchScalarGridSpec(
            num_scalar_prefetch=1,
            grid=(FF // TILE,),
            in_specs=[
                whole((REGION, WIDTH)),
                whole((REGION, WIDTH)),
                whole((WIDTH, WIDTH)),
                whole((1, WIDTH)),
                whole((REGION, WIDTH)),
                cols,
                cols,
                pl.BlockSpec((TILE, WIDTH), lambda g, ids: (tile_of(g, ids), 0)),
            ],
            out_specs=[
                whole((REGION, WIDTH)),
                whole((REGION, WIDTH)),
                whole((REGION, WIDTH)),
                whole((WIDTH, WIDTH)),
                whole((1, WIDTH)),
                sent(0), kept(0), sent(1), kept(1), sent(2), kept(2),
            ],
            scratch_shapes=[
                pltpu.VMEM((REGION, WIDTH), F32),
                pltpu.VMEM((REGION, WIDTH), BF),
                pltpu.VMEM((WIDTH, REGION), BF),
                pltpu.VMEM((REGION, WIDTH), F32),
                pltpu.VMEM((REGION, WIDTH), F32),
            ],
        ),
        out_shape=[
            struct((REGION, WIDTH)),
            struct((REGION, WIDTH), F32),
            struct((REGION, WIDTH)),
            struct((WIDTH, WIDTH)),
            struct((1, WIDTH), F32),
            half, half, half, half, half, half,
        ],
        compiler_params=params(),
        cost_estimate=cost(12_300_000_000, 30_000_000, 800_000),
        name="feed_forward",
    )(ids, tokens, attended, wo, gain, cotangent, wg, wu, wd)


GROUP = 6
COLS = GROUP * 64


def back_kernel(
    ids, window, query, keys, values, probs, attended, d_attended, out_grad,
    d_query, d_keys_t, d_values_t, d_logits,
    send_a, keep_a, send_b, keep_b, send_c, keep_c,
    window_t, slopes,
):
    group = pl.program_id(0)

    @pl.when(group == 0)
    def _():
        window_t[...] = window[...].T

    query_t = query[...].T
    d_att_t = d_attended[...].T
    lane = lax.broadcasted_iota(jnp.int32, (REGION, 128), 1)
    for pair in range(GROUP // 2):
        lanes = slice(pair * 128, pair * 128 + 128)
        halves = []
        for half in range(2):
            head = 2 * pair + half
            mine = (lane < 64) if half == 0 else (lane >= 64)
            one = jnp.where(mine, d_attended[:, lanes], jnp.zeros((), BF))
            shared = jnp.sum(
                one.astype(F32) * attended[:, lanes].astype(F32), axis=-1, keepdims=True
            )
            slot = head % 2
            slopes[slot] = mm_nt(one, values[:, lanes])
            for begin in range(0, REGION, 32):
                part = slice(begin, begin + 32)
                grad = probs[head, part].astype(F32) * (slopes[slot, part] - shared[part])
                d_logits[head, part] = grad.astype(BF)
            halves.append(mm(d_logits[head], keys[:, lanes]))
            feats = slice(head * 64, head * 64 + 64)
            d_keys_t[feats] = (mm(query_t[feats], d_logits[head]) * 0.125).astype(BF)
            d_values_t[feats] = mm(d_att_t[feats], probs[head]).astype(BF)
        d_query[:, lanes] = (jnp.where(lane < 64, halves[0], halves[1]) * 0.125).astype(BF)
    grads = (
        mm(window_t[:, :REGION], d_query[...]).astype(BF),
        mm_nt(window_t[...], d_keys_t[...]).astype(BF),
        mm_nt(window_t[...], d_values_t[...]).astype(BF),
        out_grad[...],
    )
    core = ids[0] >> 6
    flips = [ids[k] & 63 for k in range(3)]

    def put(number, outs):
        for row in range(16):
            shard = ((2 * number + group) & 3) * 16 + row
            for third in range(3):
                begin = row * 48 + third * 16
                outs[third][shard ^ flips[third]] = grads[number][begin : begin + 16]

    for number in range(4):
        away = core != number // 2

        @pl.when(away)
        def _():
            put(number, (send_a, send_b, send_c))

        @pl.when(jnp.logical_not(away))
        def _():
            put(number, (keep_a, keep_b, keep_c))


def back_call(ids, window, query, keys, values, probs, attended, d_attended, out_grad):
    cols = lambda rows: pl.BlockSpec((rows, COLS), lambda g: (0, g))
    feats = pl.BlockSpec((COLS, WINDOW), lambda g: (g, 0))
    heads = pl.BlockSpec((GROUP, REGION, WINDOW), lambda g: (g, 0, 0))
    half = struct((HALF, PIECE, COLS))
    return pl.pallas_call(
        back_kernel,
        grid=(HEADS // GROUP,),
        in_specs=[
            smem(), whole((WINDOW, WIDTH)), cols(REGION), cols(WINDOW), cols(WINDOW), heads,
            cols(REGION), cols(REGION), cols(WIDTH),
        ],
        out_specs=[cols(REGION), feats, feats, heads] + [whole((HALF, PIECE, COLS))] * 6,
        out_shape=[
            struct((REGION, WIDTH)),
            struct((WIDTH, WINDOW)),
            struct((WIDTH, WINDOW)),
            struct((HEADS, REGION, WINDOW)),
        ]
        + [half] * 6,
        scratch_shapes=[pltpu.VMEM((WIDTH, WINDOW), BF), pltpu.VMEM((2, REGION, WINDOW), F32)],
        compiler_params=params(),
        cost_estimate=cost(6_000_000_000, 30_000_000),
        name="attend_back",
    )(ids, window, query, keys, values, probs, attended, d_attended, out_grad)


ROWS_A_STEP = 16


def table_kernel(d_logits, relative, layout, out, onehot, total):
    step = pl.program_id(0)

    @pl.when(step == 0)
    def _():
        total[...] = jnp.zeros_like(total)

    bucket = lax.broadcasted_iota(jnp.int32, (32, WINDOW), 0)
    for row in range(ROWS_A_STEP):
        for offset, source in ((0, relative), (32, layout)):
            hit = source[row : row + 1, :] == bucket
            begin = row * 64 + offset
            onehot[begin : begin + 32] = jnp.where(hit, 1.0, 0.0).astype(BF)
    left = d_logits[...].reshape(HEADS * ROWS_A_STEP, WINDOW)
    total[...] += mm_nt(left, onehot[...])

    @pl.when(step == pl.num_programs(0) - 1)
    def _():
        shape = total.shape
        left_row = lax.broadcasted_iota(jnp.int32, shape, 0) % ROWS_A_STEP
        right_row = lax.broadcasted_iota(jnp.int32, shape, 1) // 64
        kept = jnp.where(left_row == right_row, total[...], 0.0)
        by_head = jnp.sum(kept.reshape(HEADS, ROWS_A_STEP, shape[1]), axis=1)
        folded = by_head[:, 0:128]
        for tile in range(1, shape[1] // 128):
            folded = folded + by_head[:, tile * 128 : tile * 128 + 128]
        out[...] = folded[:, :64] + folded[:, 64:]


def table_call(d_logits, relative, layout):
    rows = ROWS_A_STEP
    return pl.pallas_call(
        table_kernel,
        grid=(REGION // rows,),
        in_specs=[
            pl.BlockSpec((HEADS, rows, WINDOW), lambda i: (0, i, 0)),
            pl.BlockSpec((rows, WINDOW), lambda i: (i, 0)),
            pl.BlockSpec((rows, WINDOW), lambda i: (i, 0)),
        ],
        out_specs=whole((HEADS, 64)),
        out_shape=struct((HEADS, 64), F32),
        scratch_shapes=[
            pltpu.VMEM((rows * 64, WINDOW), BF),
            pltpu.VMEM((HEADS * rows, rows * 64), F32),
        ],
        compiler_params=params(),
        cost_estimate=cost(7_000_000_000, 10_000_000),
        name="table_grads",
    )(d_logits, relative, layout)


def window_kernel(place, d_query, d_keys_t, d_values_t, wq, wk, wv, own, for_row, for_core, for_chip, rest):
    full = mm(wk[...], d_keys_t[...]) + mm(wv[...], d_values_t[...])
    own[...] = (full[:, :REGION] + mm_nt(wq[...], d_query[...])).T
    rest[...] = full[:, REGION:].T
    row, odd = place[0], place[1]
    for out, begin in (
        (for_row, HALO - HALO * row),
        (for_core, 3 * HALO - HALO * odd),
        (for_chip, 2 * HALO + HALO * odd),
    ):
        out[...] = rest[pl.ds(pl.multiple_of(begin, HALO), HALO)].astype(BF)


def window_call(place, d_query, d_keys_t, d_values_t, wq, wk, wv):
    return pl.pallas_call(
        window_kernel,
        in_specs=[smem()] + [pl.BlockSpec(memory_space=pltpu.VMEM)] * 6,
        out_specs=[pl.BlockSpec(memory_space=pltpu.VMEM)] * 4,
        out_shape=[struct((REGION, WIDTH), F32)] + [struct((HALO, WIDTH))] * 3,
        scratch_shapes=[pltpu.VMEM((WINDOW - REGION, WIDTH), F32)],
        compiler_params=params(),
        cost_estimate=cost(2_300_000_000, 10_000_000),
        name="window_back",
    )(place, d_query, d_keys_t, d_values_t, wq, wk, wv)


def input_kernel(
    place, tokens, gain, index, own, d_middle, from_row, from_core, from_chip, input_grad, gain_grad
):
    row, odd = place[0], place[1]
    back = own[...]
    for received, block in ((from_row, row), (from_core, 2 + odd), (from_chip, 3 - odd)):
        picks = index[pl.ds(block, 1), :]
        chosen = lax.broadcasted_iota(jnp.int32, (REGION, HALO), 0) == picks
        back = back + mm(jnp.where(chosen, 1.0, 0.0).astype(BF), received[...])
    value = tokens[...].astype(F32)
    inverse = lax.rsqrt(jnp.mean(value * value, axis=-1, keepdims=True) + EPS)
    gain_grad[...] = jnp.sum(back * value * inverse, axis=0, keepdims=True)
    scaled = back * gain[...].astype(F32)
    shared = jnp.mean(scaled * value, axis=-1, keepdims=True)
    input_grad[...] = (
        d_middle[...] + inverse * scaled - value * (inverse * inverse * inverse) * shared
    ).astype(BF)


def input_call(place, tokens, gain, index, own, d_middle, from_row, from_core, from_chip):
    return pl.pallas_call(
        input_kernel,
        in_specs=[smem()] + [pl.BlockSpec(memory_space=pltpu.VMEM)] * 8,
        out_specs=[pl.BlockSpec(memory_space=pltpu.VMEM)] * 2,
        out_shape=[struct((REGION, WIDTH)), struct((1, WIDTH), F32)],
        compiler_params=params(),
        cost_estimate=cost(500_000_000, 6_000_000),
        name="input_back",
    )(place, tokens, gain, index, own, d_middle, from_row, from_core, from_chip)


def ffn_out_kernel(ids, *refs):
    own, other, outs = refs[0:3], refs[3:6], refs[6:9]
    step = pl.program_id(0)

    def put(sources):
        flips = [ids[k] & 31 for k in range(3)]
        for piece in range(32):
            col, row = piece // 16, piece % 16
            for k in range(2):
                block = sources[k][piece ^ flips[k]].astype(F32)
                for third in range(3):
                    begin = row * 48 + third * 16
                    outs[k][begin : begin + 16, col * 256 : col * 256 + 256] = block[
                        :, third * 256 : third * 256 + 256
                    ]
            outs[2][piece * 16 : piece * 16 + 16] = sources[2][piece ^ flips[2]].astype(F32)

    @pl.when(step < 2)
    def _():
        put(own)

    @pl.when(step >= 2)
    def _():
        put(other)


def ffn_out_call(ids, own, other):
    block = (32, PIECE, WIDTH)

    def of_own(k):
        def index(g, ids):
            return (jnp.where(g < 2, g & 1, 1) ^ ((ids[k] >> 5) & 1), 0, 0)
        return pl.BlockSpec(block, index)

    def of_other(k):
        def index(g, ids):
            return (jnp.where(g < 2, 0, g & 1) ^ ((ids[k] >> 5) & 1), 0, 0)
        return pl.BlockSpec(block, index)

    def tile(g, ids):
        core = ids[0] >> 6
        return jnp.where(g < 2, core, 1 - core) * 2 + (g & 1)

    cols = pl.BlockSpec((WIDTH, TILE), lambda g, ids: (0, tile(g, ids)))
    return pl.pallas_call(
        ffn_out_kernel,
        grid_spec=pltpu.PrefetchScalarGridSpec(
            num_scalar_prefetch=1,
            grid=(FF // TILE,),
            in_specs=[of_own(k) for k in range(3)] + [of_other(k) for k in range(3)],
            out_specs=[cols, cols, pl.BlockSpec((TILE, WIDTH), lambda g, ids: (tile(g, ids), 0))],
        ),
        out_shape=[struct((WIDTH, FF), F32), struct((WIDTH, FF), F32), struct((FF, WIDTH), F32)],
        compiler_params=params(),
        cost_estimate=cost(10_000_000, 28_000_000),
        name="feed_forward_out",
    )(ids, *own, *other)


def att_out_kernel(ids, *refs):
    own, other, outs = refs[0:3], refs[3:6], refs[6:10]
    group = pl.program_id(0)
    core = ids[0] >> 6
    flips = [ids[k] & 63 for k in range(3)]

    def put(number, sources):
        for row in range(16):
            shard = ((2 * number + group) & 3) * 16 + row
            for third in range(3):
                begin = row * 48 + third * 16
                outs[number][begin : begin + 16] = sources[third][shard ^ flips[third]].astype(F32)

    for number in range(4):
        mine = core == number // 2

        @pl.when(mine)
        def _():
            put(number, own)

        @pl.when(jnp.logical_not(mine))
        def _():
            put(number, other)


def att_out_call(ids, own, other):
    return pl.pallas_call(
        att_out_kernel,
        grid=(2,),
        in_specs=[smem()] + [whole((HALF, PIECE, COLS))] * 6,
        out_specs=[pl.BlockSpec((WIDTH, COLS), lambda g: (0, g))] * 4,
        out_shape=[struct((WIDTH, WIDTH), F32)] * 4,
        compiler_params=params(),
        cost_estimate=cost(10_000_000, 14_000_000),
        name="attend_out",
    )(ids, *own, *other)


def body(
    tokens, attn_gain, query_weight, key_weight, value_weight, output_weight, ffn_gain, gate_weight,
    up_weight, down_weight, relative_table, layout_table, cotangent, rel_bucket, layout_bucket,
    halo_index,
):
    row = lax.axis_index("row")
    col = lax.axis_index("col")
    place = jnp.stack([row, col % 2]).astype(jnp.int32)
    ids = jnp.zeros((3,), jnp.int32)
    tokens, cotangent = tokens[0], cotangent[0]
    relative, layout = rel_bucket[0], layout_bucket[0]
    index = halo_index[0, 0]
    gain_one, gain_two = attn_gain[None], ffn_gain[None]
    columns = lax.axis_size("col")
    row_pairs = [(0, 1), (1, 0)]
    core_pairs = [(c, c ^ 1) for c in range(columns)]
    chip_pairs = [p for c in range(1, columns - 1, 2) for p in ((c, c + 1), (c + 1, c))]

    def exchange(for_row, for_core, for_chip):
        return (
            lax.ppermute(for_row, "row", row_pairs),
            lax.ppermute(for_core, "col", core_pairs),
            lax.ppermute(for_chip, "col", chip_pairs),
        )

    normed, *sends = norm_call(place, tokens, gain_one, index)
    received = exchange(*sends)
    bias = bias_call(packed_table(relative_table, layout_table), relative, layout)
    window, query, keys, values, probs, attended = attend_call(
        place, normed, *received, query_weight, key_weight, value_weight, bias, 4
    )
    layer_out, d_middle, d_attended, out_grad, gain_two_grad, *ffn_parts = ffn_call(
        ids, tokens, attended, output_weight, gain_two, cotangent, gate_weight, up_weight, down_weight
    )
    d_query, d_keys_t, d_values_t, d_logits, *att_parts = back_call(
        ids, window, query, keys, values, probs, attended, d_attended, out_grad
    )
    tables = table_call(d_logits, relative, layout)
    own, *returns = window_call(
        place, d_query, d_keys_t, d_values_t, query_weight, key_weight, value_weight
    )
    returned = exchange(*returns)
    input_grad, gain_one_grad = input_call(
        place, tokens, gain_one, index, own, d_middle, *returned
    )
    small = jnp.concatenate([gain_one_grad, gain_two_grad, tables.reshape(1, WIDTH)], axis=0)
    high = small.astype(BF)
    low = (small - high.astype(F32)).astype(BF)
    ffn_parts, att_parts, high, low = lax.psum((ffn_parts, att_parts, high, low), ("row", "col"))
    small = high.astype(F32) + low.astype(F32)
    gate_grad, up_grad, down_grad = ffn_out_call(ids, ffn_parts[1::2], ffn_parts[0::2])
    query_grad, key_grad, value_grad, output_grad = att_out_call(
        ids, att_parts[1::2], att_parts[0::2]
    )
    tables = small[2].reshape(HEADS, 64)
    return (
        layer_out[None], input_grad[None], small[0], query_grad, key_grad, value_grad, output_grad,
        small[1], gate_grad, up_grad, down_grad, tables[:, :32].T, tables[:, 32:].T,
    )


def solution(mesh):
    tokens = P("row", "col", None)
    whole_array = P()
    return jax.shard_map(
        body,
        mesh=mesh,
        in_specs=(tokens,) + (whole_array,) * 11 + (tokens,) * 3 + (P("row", "col", None, None),),
        out_specs=(tokens, tokens) + (whole_array,) * 11,
        check_vma=False,
    )
```

time: 617 us -> 295 us (0.48)
  matrix products: 138 us -> 0 us
  local copies, waits for them, and re-layouts: 135 us -> 6.94 us
  Pallas kernels: 0 us -> 120 us
  waiting for transfers between devices: 135 us -> 67.8 us
  other arithmetic: 53.2 us -> 2.11 us
  starting transfers between devices: 56.3 us -> 12.1 us
  blocking collectives: 77.2 us -> 70.5 us
    dot_general x31 -> x0, matrix products: 138 us -> none  [the longest x7 27.3 us: matmul_tn(): lax.dot_general(left, right, (((0,), (0,)), ((), ())), preferred_element_...]
    pallas_call x0 -> x10, Pallas kernels: none -> 120 us  [the longest x1 24.2 us: ffn_call(): pl.pallas_call(ffn_kernel, grid_spec=pltpu.PrefetchScalarGridSpec(num_sca...]
    psum x1, waiting for transfers between devices: 135 us -> 67.7 us  [body(): lax.psum((ffn_parts, att_parts, high, low), ('row', 'col'))]
    ppermute x16 -> x6, starting transfers between devices: 56.3 us -> 12.1 us  [the longest x2 7.35 us: exchange(): lax.ppermute(for_chip, 'col', chip_pairs)]
    dot_general x2 -> x0, local copies, waits for them, and re-layouts: 34.9 us -> none  [the longest x1 17.5 us: body(): jnp.einsum('qkb,bh->hqk', rel_onehot, relative_table, preferred_element_t...]
    unnamed x125 -> x20, local copies, waits for them, and re-layouts: 35.3 us -> 1.46 us
    scatter-add x8 -> x0, other arithmetic: 31.1 us -> none  [the longest x4 15.6 us: body(): d_keys = d_keys.at[picks[number]].add(returned[0])]
    convert_element_type x11 -> x0, local copies, waits for them, and re-layouts: 27.2 us -> none  [the longest x1 13.5 us: body(): (probs * (d_probs - jnp.sum(probs * d_probs, axis=-1, keepdims=True))).as...]
  transfers between devices with their start and end apart: 17 -> 7, of which waited for: 1 -> 1; matrix products, arithmetic and copies ran while one was open for 30% -> 2% of each run, Pallas kernels for 0% -> 14%
where the time goes in v1:
time: 295 us; the launch traced here: 294 us
  Pallas kernels  120 us (41%)
  blocking collectives  70.5 us (24%)
  waiting for transfers between devices  67.8 us (23%)
  between operations  14.2 us (5%)
  starting transfers between devices  12.1 us (4%)
  local copies, waits for them, and re-layouts  6.94 us (2%)
    psum x1, blocking collectives, body(): lax.psum((ffn_parts, att_parts, high, low), ('row', 'col'))  70.5 us
    psum x1, waiting for transfers between devices, body(): lax.psum((ffn_parts, att_parts, high, low), ('row', 'col'))  67.7 us
    pallas_call x1, Pallas kernels, ffn_call(): pl.pallas_call(ffn_kernel, grid_spec=pltpu.PrefetchScalarGridSpec(num_sca...  24.2 us
    pallas_call x1, Pallas kernels, table_call(): pl.pallas_call(table_kernel, grid=(REGION // rows,), in_specs=[pl.BlockSp...  21.8 us
    pallas_call x1, Pallas kernels, back_call(): pl.pallas_call(back_kernel, grid=(HEADS // GROUP,), in_specs=[smem(), who...  19.1 us
    pallas_call x1, Pallas kernels, attend_call(): pl.pallas_call(attend_kernel, grid=(count,), out_shape=(struct((WINDOW, W...  14.7 us
    pallas_call x1, Pallas kernels, ffn_out_call(): pl.pallas_call(ffn_out_kernel, grid_spec=pltpu.PrefetchScalarGridSpec(num...  11.3 us
    pallas_call x1, Pallas kernels, bias_call(): pl.pallas_call(bias_kernel, grid=(REGION // block,), out_shape=struct((HE...  10 us
  transfers between devices with their start and end apart: 7, of which 1 were waited for; matrix products, arithmetic and copies ran while one was open for 2% of the time, Pallas kernels for 14%

profile of v1, /device:TPU:1, one launch (start us, length us, event | category | flops | bytes accessed | tf_op | source)
XLA Modules:
  0.0 294.1 jit_solution(1180982672494178785)
XLA Ops:
  7.2 0.0 copy-start.7
  7.2 0.0 all-reduce.4.cloned.1.call-start
  7.3 1.3 broadcast_in_dim.19.gain
  8.5 0.7 pad_add_fusion.place
  9.2 2.4 norm_one.1
  11.6 3.6 %collective-permute-start = (bf16[96,768]{1,0:T(8,128)(2,1)}, bf16[96,768]{1,0:T(8,128)(2,1)S(1)}, u32[]{:S(2)}, u32[]{:S(2)}) collective-permute-start(bf16[96,768]{1,0:T(8,128)(2,1)} %get-tuple-element.58), channel_id=1, source_target_pairs={{0,64},{64,0},{1,65},{65,1},{2,66},{66,2},{3,67},{67,3},{4,68},{68... | collective-permute-start | bytes 442376 | tf_op jit(solution)/shard_map/ppermute | solution.py:688
  15.2 1.0 collective-permute-start.1
  16.1 3.4 %collective-permute-start.2 = (bf16[96,768]{1,0:T(8,128)(2,1)}, bf16[96,768]{1,0:T(8,128)(2,1)S(1)}, u32[]{:S(2)}, u32[]{:S(2)}) collective-permute-start(bf16[96,768]{1,0:T(8,128)(2,1)} %get-tuple-element.60), channel_id=1, source_target_pairs={{1,2},{2,1},{3,4},{4,3},{5,6},{6,5},{7,8},{8,7},{9,10},{10,9},{11,... | collective-permute-start | bytes 442376 | tf_op jit(solution)/shard_map/ppermute | solution.py:690
  19.7 0.6 broadcast_in_dim.22.gain
  20.3 0.1 reshape.38
  20.4 0.1 reshape.37
  20.5 0.8 broadcast_in_dim.21.table
  21.2 10.0 %bias.1 = f32[12,384,768]{2,1,0:T(8,128)} custom-call(s32[48,8,128]{2,1,0:T(8,128)} %broadcast_in_dim.21.table, s32[384,768]{1,0:T(8,128)} %bitcast.19, s32[384,768]{1,0:T(8,128)} %bitcast.21), custom_call_target="tpu_custom_call" | custom-call | flops 100000000 | bytes 17000000 | tf_op jit(solution)/shard_map/bias/pallas_call | solution.py:114
  31.3 0.0 collective-permute-done.from_row
  31.3 0.0 collective-permute-done.1.from_core
  31.3 0.0 copy-start.1
  31.3 0.0 collective-permute-done.2.from_chip
  31.3 0.0 copy-start.2
  31.3 0.6 copy-done
  31.9 0.0 copy-done.1
  32.0 0.0 copy-done.2
  32.0 14.7 %attend.1 = (bf16[768,768]{1,0:T(8,128)(2,1)}, bf16[384,768]{1,0:T(8,128)(2,1)}, bf16[768,768]{1,0:T(8,128)(2,1)}, bf16[768,768]{1,0:T(8,128)(2,1)}, bf16[12,384...) custom-call(s32[2]{0:T(128)} %pad_add_fusion.place, bf16[384,768]{1,0:T(8,128)(2,1)} %get-tuple-element.57.normed, ...), custom_call_target="tpu_custom_call" | custom-call | flops 3500000000 | bytes 30000000 | tf_op jit(solution)/shard_map/attend/pallas_call | solution.py:184
  46.7 0.5 broadcast_7_ids.2.ids
  47.2 24.2 %feed_forward.1 = (bf16[384,768]{1,0:T(8,128)(2,1)}, f32[384,768]{1,0:T(8,128)}, bf16[384,768]{1,0:T(8,128)(2,1)}, bf16[768,768]{1,0:T(8,128)(2,1)}, f32[1,768]{...) custom-call(s32[3]{0:T(128)} %broadcast_7_ids.2.ids, ...), custom_call_target="tpu_custom_call" | custom-call | flops 12300000256 | bytes 30000000 | tf_op jit(solution)/shard_map/feed_forward/pallas_call | solution.py:320
  71.4 19.1 %attend_back.1 = (bf16[384,768]{1,0:T(8,128)(2,1)}, bf16[768,768]{1,0:T(8,128)(2,1)}, bf16[768,768]{1,0:T(8,128)(2,1)}, bf16[12,384,768]{2,1,0:T(8,128)(2,1)}, b...) custom-call(s32[3]{0:T(128)} %broadcast_7_ids.2.ids, ...), custom_call_target="tpu_custom_call" | custom-call | flops 6000000000 | bytes 30000000 | tf_op jit(solution)/shard_map/attend_back/pallas_call | solution.py:438
  90.5 0.0 all-reduce.4.cloned.1.call-update
  90.5 6.8 %window_back.1 = (f32[384,768]{1,0:T(8,128)}, bf16[96,768]{1,0:T(8,128)(2,1)}, bf16[96,768]{1,0:T(8,128)(2,1)}, bf16[96,768]{1,0:T(8,128)(2,1)}) custom-call(s32[2]{0:T(128)} %pad_add_fusion.place, bf16[384,768]{1,0:T(8,128)(2,1)} %get-tuple-element.70.d_query, bf16[768,768]{1,0:T(8,128)(2,1)} %get-tuple-element.71.d_keys_t, ...), custom_call_target="tpu_custom_call" | custom-call | flops 2300000000 | bytes 10000000 | tf_op jit(solution)/shard_map/window_back/pallas_call | solution.py:528
  97.3 0.2 collective-permute-start.3
  97.5 0.0 collective-permute-start.4
  97.5 3.9 %collective-permute-start.5 = (bf16[96,768]{1,0:T(8,128)(2,1)}, bf16[96,768]{1,0:T(8,128)(2,1)S(1)}, u32[]{:S(2)}, u32[]{:S(2)}) collective-permute-start(bf16[96,768]{1,0:T(8,128)(2,1)} %get-tuple-element.77), channel_id=1, source_target_pairs={{1,2},{2,1},{3,4},{4,3},{5,6},{6,5},{7,8},{8,7},{9,10},{10,9},{11,... | collective-permute-start | bytes 442376 | tf_op jit(solution)/shard_map/ppermute | solution.py:690
  101.4 21.8 %table_grads.1 = f32[12,64]{1,0:T(8,128)} custom-call(bf16[12,384,768]{2,1,0:T(8,128)(2,1)} %get-tuple-element.81.d_logits, s32[384,768]{1,0:T(8,128)} %bitcast.20, s32[384,768]{1,0:T(8,128)} %bitcast.22), custom_call_target="tpu_custom_call" | custom-call | flops 7000000000 | bytes 10000000 | tf_op jit(solution)/shard_map/table_grads/pallas_call | solution.py:494
  123.2 0.8 reshape.39
  124.0 0.0 collective-permute-done.3.from_row
  124.0 0.0 collective-permute-done.4.from_core
  124.0 0.0 collective-permute-done.5.from_chip
  124.0 0.6 copy-done.3
  124.7 0.1 copy-done.4
  124.7 0.0 copy-done.5
  124.8 3.9 %input_back.1 = (bf16[384,768]{1,0:T(8,128)(2,1)}, f32[1,768]{1,0:T(1,128)}) custom-call(s32[2]{0:T(128)} %pad_add_fusion.place, bf16[384,768]{1,0:T(8,128)(2,1)} %bitcast.25, bf16[1,768]{1,0:T(2,128)(2,1)} %broadcast_in_dim.19.gain, s32[4,96]{1,0:T(4,128)} %bitcast.27, f32[384,768]{1,0:T(8,128)} %get-tuple-element.73.own, ...), custom_call_target="tpu_custom_call" | custom-call | flops 500000000 | bytes 6000000 | tf_op jit(solution)/shard_map/input_back/pallas_call | solution.py:560
  128.7 0.7 subtract_convert_fusion
  129.4 0.7 fusion
  130.1 70.5 %all-reduce = (bf16[3,768]{1,0:T(4,128)(2,1)S(1)}, bf16[3,768]{1,0:T(4,128)(2,1)S(1)}) all-reduce(bf16[3,768]{1,0:T(4,128)(2,1)S(1)} %subtract_convert_fusion, bf16[3,768]{1,0:T(4,128)(2,1)S(1)} %fusion), channel_id=1, replica_groups=mesh['row'=2,'col'=64] {'row','col'}, use_global_device_ids=true, to_apply=%region_1.2 | all-reduce | flops 4608 | bytes 18432 | tf_op jit(solution)/shard_map/psum | solution.py:716
  200.6 0.6 slice_reduce_fusion
  201.2 0.1 reshape_squeeze.3
  201.2 0.7 slice_bitcast_fusion
  201.9 67.7 %all-reduce.4.cloned.1.call-done = (bf16[64,16,384]{2,1,0:T(8,128)(2,1)}, bf16[64,16,384]{2,1,0:T(8,128)(2,1)}, bf16[64,16,384]{2,1,0:T(8,128)(2,1)}, bf16[64,16...) async-done(((bf16[64,16,384]{2,1,0:T(8,128)(2,1)}, ...) | async-done | bytes 14155792 | tf_op jit(solution)/shard_map/psum | solution.py:716
  269.6 6.3 %attend_out.1 = (f32[768,768]{1,0:T(8,128)}, f32[768,768]{1,0:T(8,128)}, f32[768,768]{1,0:T(8,128)}, f32[768,768]{1,0:T(8,128)}) custom-call(s32[3]{0:T(128)} %broadcast_7_ids.2.ids, bf16[64,16,384]{2,1,0:T(8,128)(2,1)} %get-tuple-element.106.refs_0_, bf16[64,16,384]{2,1,0:T(8,128)(2,1)} %get-tuple-element.107.refs_1_, ...), custom_call_target="tpu_custom_call" | custom-call | flops 10000000 | bytes 14000000 | tf_op jit(solution)/shard_map/attend_out/pallas_call | solution.py:656
  276.0 11.3 %feed_forward_out.1 = (f32[768,2048]{1,0:T(8,128)}, f32[768,2048]{1,0:T(8,128)}, f32[2048,768]{1,0:T(8,128)}) custom-call(s32[3]{0:T(128)} %broadcast_7_ids.2.ids, bf16[64,16,768]{2,1,0:T(8,128)(2,1)} %get-tuple-element.112.refs_0_, bf16[64,16,768]{2,1,0:T(8,128)(2,1)} %get-tuple-element.113.refs_1_, bf16[64,16,768]{2,1,0:T(8,128)(2,1)} %get-tuple-element.114.refs_2_, ...), custom_call_target="tpu_custom_call" | custom-call | flops 10000000 | bytes 28000000 | tf_op jit(solution)/shard_map/feed_forward_out/pallas_call | solution.py:615
  (21 shorter events, 0.1 us)
Async XLA Ops:
  7.2 12.4 %copy-start.7 = (bf16[32,12]{0,1:T(8,128)(2,1)S(1)}, bf16[32,12]{0,1:T(8,128)(2,1)}, u32[]{:S(2)}) copy-start(bf16[32,12]{0,1:T(8,128)(2,1)} %param.26) | copy-start | bytes 2308
  7.2 12.4 %copy-start.8 = (bf16[32,12]{0,1:T(8,128)(2,1)S(1)}, bf16[32,12]{0,1:T(8,128)(2,1)}, u32[]{:S(2)}) copy-start(bf16[32,12]{0,1:T(8,128)(2,1)} %param.27) | copy-start | bytes 2308
  7.2 12.5 %copy-start.9 = (bf16[768]{0:T(1024)(128)(2,1)S(1)}, bf16[768]{0:T(1024)(128)(2,1)}, u32[]{:S(2)}) copy-start(bf16[768]{0:T(1024)(128)(2,1)} %param.22) | copy-start | bytes 4612
  7.2 262.4 %all-reduce.4.cloned.1.call-start = ((), (), s32[]{:S(2)}) async-start(), calls=%async_computation | async-start | bytes 28311552 | tf_op jit(solution)/shard_map/psum | solution.py:716
  11.6 19.7 %collective-permute-start = (bf16[96,768]{1,0:T(8,128)(2,1)}, bf16[96,768]{1,0:T(8,128)(2,1)S(1)}, u32[]{:S(2)}, u32[]{:S(2)}) collective-permute-start(bf16[96,768]{1,0:T(8,128)(2,1)} %get-tuple-element.58), channel_id=1, source_target_pairs={{0,64},{64,0},{1,65},{65,1},{2,66},{66,2},{3,67},{67,3},{4,68},{68... | collective-permute-start | bytes 442376 | tf_op jit(solution)/shard_map/ppermute | solution.py:688
  15.2 16.1 %collective-permute-start.1 = (bf16[96,768]{1,0:T(8,128)(2,1)}, bf16[96,768]{1,0:T(8,128)(2,1)S(1)}, u32[]{:S(2)}, u32[]{:S(2)}) collective-permute-start(bf16[96,768]{1,0:T(8,128)(2,1)} %get-tuple-element.59), channel_id=1, source_target_pairs={{0,1},{1,0},{2,3},{3,2},{4,5},{5,4},{6,7},{7,6},{8,9},{9,8},{10,11... | collective-permute-start | bytes 442376 | tf_op jit(solution)/shard_map/ppermute | solution.py:689
  16.1 15.2 %collective-permute-start.2 = (bf16[96,768]{1,0:T(8,128)(2,1)}, bf16[96,768]{1,0:T(8,128)(2,1)S(1)}, u32[]{:S(2)}, u32[]{:S(2)}) collective-permute-start(bf16[96,768]{1,0:T(8,128)(2,1)} %get-tuple-element.60), channel_id=1, source_target_pairs={{1,2},{2,1},{3,4},{4,3},{5,6},{6,5},{7,8},{8,7},{9,10},{10,9},{11,... | collective-permute-start | bytes 442376 | tf_op jit(solution)/shard_map/ppermute | solution.py:690
  31.3 0.7 copy-start
  31.3 0.7 copy-start.1
  31.3 0.7 copy-start.2
  97.3 26.7 %collective-permute-start.3 = (bf16[96,768]{1,0:T(8,128)(2,1)}, bf16[96,768]{1,0:T(8,128)(2,1)S(1)}, u32[]{:S(2)}, u32[]{:S(2)}) collective-permute-start(bf16[96,768]{1,0:T(8,128)(2,1)} %get-tuple-element.75), channel_id=1, source_target_pairs={{0,64},{64,0},{1,65},{65,1},{2,66},{66,2},{3,67},{67,3},{4,68},{68... | collective-permute-start | bytes 442376 | tf_op jit(solution)/shard_map/ppermute | solution.py:688
  97.5 26.5 %collective-permute-start.4 = (bf16[96,768]{1,0:T(8,128)(2,1)}, bf16[96,768]{1,0:T(8,128)(2,1)S(1)}, u32[]{:S(2)}, u32[]{:S(2)}) collective-permute-start(bf16[96,768]{1,0:T(8,128)(2,1)} %get-tuple-element.76), channel_id=1, source_target_pairs={{0,1},{1,0},{2,3},{3,2},{4,5},{5,4},{6,7},{7,6},{8,9},{9,8},{10,11... | collective-permute-start | bytes 442376 | tf_op jit(solution)/shard_map/ppermute | solution.py:689
  97.5 26.5 %collective-permute-start.5 = (bf16[96,768]{1,0:T(8,128)(2,1)}, bf16[96,768]{1,0:T(8,128)(2,1)S(1)}, u32[]{:S(2)}, u32[]{:S(2)}) collective-permute-start(bf16[96,768]{1,0:T(8,128)(2,1)} %get-tuple-element.77), channel_id=1, source_target_pairs={{1,2},{2,1},{3,4},{4,3},{5,6},{6,5},{7,8},{8,7},{9,10},{10,9},{11,... | collective-permute-start | bytes 442376 | tf_op jit(solution)/shard_map/ppermute | solution.py:690
  124.0 0.7 copy-start.3
  124.0 0.7 copy-start.4
  124.0 0.7 copy-start.5
  124.8 3.9 %copy-start.6 = (f32[1,768]{1,0:T(1,128)S(1)}, f32[1,768]{1,0:T(1,128)}, u32[]{:S(2)}) copy-start(f32[1,768]{1,0:T(1,128)} %get-tuple-element.80) | copy-start | bytes 9220
Sparse Core Ops, SparseCore 0:
  90.6 178.9 all-reduce.3
